TPU v7x, 128 devices: a whole 4x4x4 slice. The times are simulated.
128 devices in a mesh: node: 8 (over x, z_hi), local: 16 (over y, z_lo, core).
Axes of the slice: x: 4, y: 4, z: 4 (z_hi: 2, z_lo: 2; z = z_hi * 2 + z_lo), core: 2. Of those that a mesh axis runs over, the one named last changes fastest.
Arguments:
- context: bfloat16 [8192, 7168], P(('node', 'local')), may hold values from -6 to 6
- cotangent: bfloat16 [8192, 7168], P(('node', 'local')), may hold values from -6 to 6
- weight: bfloat16 [7168, 7168], P(None, 'local'), may hold values from -6 to 6
Outputs:
- input_grad: bfloat16 [8192, 7168], P(('node', 'local'))
- new_weight: float32 [8, 7168, 7168], P('node', None, 'local')
All inputs are finite; a program needn't handle non-finite values.
Results may differ from a plain program's by a relative error of at most 0.00165.
Values may be sent and summed in bfloat16 or wider, within the bound.
No kernel may reach another device: no remote copies, remote signals or barrier semaphores. Data moves between devices by JAX's collectives and lax.ppermute only.
A program may use at most 192 MiB of HBM per device.

v0:
```python
import jax
import jax.numpy as jnp
from jax import lax
from jax.sharding import PartitionSpec as P


def passed_along(block, axis, distance):
    devices = range(lax.axis_size(axis))
    route = [((i - distance) % len(devices), i) for i in devices]
    return lax.ppermute(block, axis, route)


def decode(code, low, span):
    return low + code.astype(jnp.float32) * span / 255.0


def body(context, cotangent, weight):
    scale = context.shape[1] ** (-0.5)
    cot_block = lax.all_to_all(cotangent, "local", split_axis=1, concat_axis=0, tiled=True)
    rows = cot_block
    input_grad = lax.psum_scatter(
        jnp.dot(rows, weight.T, preferred_element_type=jnp.float32) * scale,
        "local",
        scatter_dimension=0,
        tiled=True,
    ).astype(jnp.bfloat16)
    rows = cot_block
    grad = (
        lax.dot_general(
            lax.all_gather(context, "local", axis=0, tiled=True),
            rows,
            (((0,), (0,)), ((), ())),
            preferred_element_type=jnp.float32,
        )
        * scale
    )
    diff = -0.25 * grad
    low = jnp.min(diff, axis=1, keepdims=True)
    span = jnp.max(diff, axis=1, keepdims=True) - low
    code = (255.0 * (diff - low) / span).astype(jnp.bfloat16)
    own = decode(code, low, span)
    lower = (
        passed_along(code, "node", 1),
        passed_along(low.astype(jnp.bfloat16), "node", 1).astype(low.dtype),
        passed_along(span.astype(jnp.bfloat16), "node", 1).astype(span.dtype),
    )
    upper = (
        passed_along(code, "node", -1),
        passed_along(low.astype(jnp.bfloat16), "node", -1).astype(low.dtype),
        passed_along(span.astype(jnp.bfloat16), "node", -1).astype(span.dtype),
    )
    below = decode(lower[0], lower[1], lower[2])
    above = decode(upper[0], upper[1], upper[2])
    new_weight = weight.astype(jnp.float32) + (below + own + above) / 3.0
    return (input_grad, new_weight[None])


def solution(mesh):
    return jax.shard_map(
        body,
        mesh=mesh,
        in_specs=(P(("node", "local"), None), P(("node", "local"), None), P(None, "local")),
        out_specs=(P(("node", "local"), None), P("node", None, "local")),
        check_vma=False,
    )
```

profile of v0, /device:TPU:1, one launch (start us, length us, event | category | flops | bytes accessed | tf_op | source)
XLA Modules:
  0.0 701.1 jit_solution(7404440819478735655)
XLA Ops:
  7.2 0.0 all-gather.2.cloned.1.call-start
  7.2 0.7 all-gather.2.cloned.1.call-update
  7.9 0.0 reduce-scatter.2.cloned.1.call-start
  7.9 2.4 all_to_all.14
  10.3 0.6 copy.5
  10.9 29.5 %all_to_all.19 = bf16[64,16,448]{2,0,1:T(8,128)(2,1)S(1)} all-to-all(bf16[64,16,448]{2,0,1:T(8,128)(2,1)S(1)} %copy.5), channel_id=1, replica_groups=mesh['node'=8,'local'=16] {'local'}, dimensions={1} | all-to-all | bytes 1835008 | tf_op jit(solution)/shard_map/all_to_all | solution.py:19
  40.4 16.7 %convolution_multiply_fusion = f32[1024,7168]{1,0:T(8,128)} fusion(bf16[1024,448]{1,0:T(8,128)(2,1)S(1)} %bitcast.13, bf16[7168,448]{0,1:T(8,128)(2,1)} %param.5), kind=kOutput, calls=%fused_computation | convolution fusion | flops 6584008704 | bytes 36700160 | tf_op jit(solution)/shard_map/dot_general | solution.py:22
  57.1 0.0 reduce-scatter.2.cloned.1.call-update
  57.1 45.8 %all-gather.2.cloned.1.call-done = bf16[1024,7168]{1,0:T(8,128)(2,1)} async-done(((bf16[64,7168]{1,0:T(8,128)(2,1)}), bf16[1024,7168]{1,0:T(8,128)(2,1)}) %all-gather.2.cloned.1.call-update) | async-done | bytes 14680080 | tf_op jit(solution)/shard_map/all_gather | solution.py:30
  102.9 13.8 %multiply_reduce_fusion.1 = (f32[7168]{0:T(1024)S(1)}, f32[7168]{0:T(1024)S(1)}, f32[7168,448]{0,1:T(8,128)}) fusion(bf16[1024,7168]{1,0:T(8,128)(2,1)} %all-gather.2.cloned.1.call-done, bf16[1024,448]{1,0:T(8,128)(2,1)S(1)} %bitcast.14), kind=kOutput, calls=%fused_computation.4 | convolution fusion | flops 6586288128 | bytes 28499968 | tf_op jit(solution)/shard_map/dot_general | solution.py:29
  116.7 9.5 %divide_convert_fusion = bf16[7168,448]{0,1:T(8,128)(2,1)} fusion(f32[7168,448]{0,1:T(8,128)} %get-tuple-element.7, f32[7168]{0:T(1024)S(1)} %get-tuple-element.5, f32[7168]{0:T(1024)S(1)} %get-tuple-element.2), kind=kLoop, calls=%fused_computation.2 | loop fusion | flops 16056320 | bytes 19324928 | tf_op jit(solution)/shard_map/convert_element_type | solution.py:40
  126.2 5.5 collective-permute-start.4
  131.7 0.0 collective-permute-start.1
  131.7 5.3 collective-permute-start.5
  137.0 0.1 collective-permute-start.3
  137.1 3.0 collective-permute-start.2
  140.1 411.7 %collective-permute-done.5 = bf16[7168,1]{0,1:T(2,128)(2,1)S(1)} collective-permute-done((bf16[7168,1]{0,1:T(2,128)(2,1)S(1)}, bf16[7168,1]{0,1:T(2,128)(2,1)S(1)}, u32[]{:S(2)}, u32[]{:S(2)}) %collective-permute-start.5) | collective-permute-done | bytes 14368 | tf_op jit(solution)/shard_map/ppermute | solution.py:10
  551.8 0.0 collective-permute-start
  551.9 0.9 collective-permute-done.3
  552.8 0.0 collective-permute-done.2
  552.8 5.7 collective-permute-done
  558.5 0.0 collective-permute-done.4
  558.6 0.0 collective-permute-done.1
  558.6 15.2 %add_bitcast_fusion = f32[1,7168,448]{1,2,0:T(8,128)} fusion(bf16[7168,448]{0,1:T(8,128)(2,1)S(1)} %collective-permute-done.4, bf16[7168,448]{0,1:T(8,128)(2,1)S(1)} %collective-permute-done.1, bf16[7168,448]{0,1:T(8,128)(2,1)} %param.5, f32[7168]{0:T(1024)S(1)} %bitcast.15, f32[7168]{0:T(1024)S(1)} %bitcast.16, f32[7168]{0:T(1024)S(1)} %bitcast.17, ...), kind=kLoop, calls=%fused_computation.1 | loop fusion | flops 70647808 | bytes 45129728 | tf_op jit(solution)/shard_map/broadcast_in_dim | solution.py:55
  573.7 118.0 %reduce-scatter.2.cloned.1.call-done = f32[64,7168]{1,0:T(8,128)} async-done(((f32[1024,7168]{1,0:T(8,128)}), f32[64,7168]{1,0:T(8,128)}) %reduce-scatter.2.cloned.1.call-update) | async-done | bytes 1835024 | tf_op jit(solution)/shard_map/reduce_scatter | solution.py:21
  691.7 2.5 convert_element_type.52
  (7 shorter events, 0.2 us)
Async XLA Ops:
  7.2 95.7 %all-gather.2.cloned.1.call-start = ((), (), s32[]{:S(2)}) async-start(), calls=%async_computation.3 | async-start | bytes 15597568 | tf_op jit(solution)/shard_map/all_gather | solution.py:30
  7.9 683.8 %reduce-scatter.2.cloned.1.call-start = ((), (), s32[]{:S(2)}) async-start(), calls=%async_computation.2 | async-start | bytes 31195136 | tf_op jit(solution)/shard_map/reduce_scatter | solution.py:21
  126.2 432.4 %collective-permute-start.4 = (bf16[7168,448]{0,1:T(8,128)(2,1)}, bf16[7168,448]{0,1:T(8,128)(2,1)S(1)}, u32[]{:S(2)}, u32[]{:S(2)}) collective-permute-start(bf16[7168,448]{0,1:T(8,128)(2,1)} %divide_convert_fusion), channel_id=1, source_target_pairs={{16,0},{32,16},{48,32},{64,48},{80,64},{96,80},{112,96},{0,112},{1... | collective-permute-start | bytes 19267592 | tf_op jit(solution)/shard_map/ppermute | solution.py:10
  131.7 426.9 %collective-permute-start.1 = (bf16[7168,448]{0,1:T(8,128)(2,1)}, bf16[7168,448]{0,1:T(8,128)(2,1)S(1)}, u32[]{:S(2)}, u32[]{:S(2)}) collective-permute-start(bf16[7168,448]{0,1:T(8,128)(2,1)} %divide_convert_fusion), channel_id=1, source_target_pairs={{112,0},{0,16},{16,32},{32,48},{48,64},{64,80},{80,96},{96,112},{1... | collective-permute-start | bytes 19267592 | tf_op jit(solution)/shard_map/ppermute | solution.py:10
  131.7 420.1 %collective-permute-start.5 = (bf16[7168,1]{0,1:T(2,128)(2,1)S(1)}, bf16[7168,1]{0,1:T(2,128)(2,1)S(1)}, u32[]{:S(2)}, u32[]{:S(2)}) collective-permute-start(bf16[7168,1]{0,1:T(2,128)(2,1)S(1)} %convert_element_type.59), channel_id=1, source_target_pairs={{16,0},{32,16},{48,32},{64,48},{80,64},{96,80},{112,96},{0,112},{1... | collective-permute-start | bytes 43016 | tf_op jit(solution)/shard_map/ppermute | solution.py:10
  137.0 415.7 %collective-permute-start.3 = (bf16[7168,1]{0,1:T(2,128)(2,1)S(1)}, bf16[7168,1]{0,1:T(2,128)(2,1)S(1)}, u32[]{:S(2)}, u32[]{:S(2)}) collective-permute-start(bf16[7168,1]{0,1:T(2,128)(2,1)S(1)} %convert_element_type.55), channel_id=1, source_target_pairs={{16,0},{32,16},{48,32},{64,48},{80,64},{96,80},{112,96},{0,112},{1... | collective-permute-start | bytes 43016 | tf_op jit(solution)/shard_map/ppermute | solution.py:10
  137.1 415.6 %collective-permute-start.2 = (bf16[7168,1]{0,1:T(2,128)(2,1)S(1)}, bf16[7168,1]{0,1:T(2,128)(2,1)S(1)}, u32[]{:S(2)}, u32[]{:S(2)}) collective-permute-start(bf16[7168,1]{0,1:T(2,128)(2,1)S(1)} %convert_element_type.59), channel_id=1, source_target_pairs={{112,0},{0,16},{16,32},{32,48},{48,64},{64,80},{80,96},{96,112},{1... | collective-permute-start | bytes 43016 | tf_op jit(solution)/shard_map/ppermute | solution.py:10
  551.8 6.7 collective-permute-start
Sparse Core Ops, SparseCore 0:
  9.7 93.1 all-gather.1
  105.3 586.3 reduce-scatter.1
where the time goes:
time: 701 us
  waiting for transfers between devices  583 us (83%)
  matrix products  30.5 us (4%)
  blocking collectives  29.5 us (4%)
  other arithmetic  27.3 us (4%)
  between operations  14.1 us (2%)
  starting transfers between devices  14 us (2%)
    ppermute x6, waiting for transfers between devices, passed_along(): return lax.ppermute(block, axis, route)  418 us
    reduce_scatter x1, waiting for transfers between devices, body(): lax.psum_scatter(jnp.dot(rows, weight.T, preferred_element_type=jnp.float...  118 us
    all_gather x1, waiting for transfers between devices, body(): lax.all_gather(context, 'local', axis=0, tiled=True)  45.8 us
    all_to_all x1, blocking collectives, body(): lax.all_to_all(cotangent, 'local', split_axis=1, concat_axis=0, tiled=True)  29.5 us
    dot_general x1, matrix products, body(): jnp.dot(rows, weight.T, preferred_element_type=jnp.float32) * scale  16.7 us
    broadcast_in_dim x1, other arithmetic, body(): return (input_grad, new_weight[None])  15.2 us
  transfers between devices with their start and end apart: 8, of which 5 were waited for; matrix products, arithmetic and copies ran while one was open for 8% of the time, Pallas kernels for 0%

commit v1 on v0

v1 whole, which is shorter than its diff:
```python
import jax
import jax.numpy as jnp
from jax import lax
from jax.experimental import pallas as pl
from jax.experimental.pallas import tpu as pltpu
from jax.sharding import Mesh, PartitionSpec as P

AXES = ("x", "zh", "y", "zl", "c")
SIZES = (4, 2, 4, 2, 2)
LOCAL = ("y", "zl", "c")

PLAN = (
    (1024, False, "pqz"),
    (1024, False, "pqz"),
    (1024, False, "qpz"),
    (1024, False, "pqz"),
    (1024, True, "zqp"),
    (1024, False, "qpz"),
    (1024, True, "zpq"),
)
SUMS = ((1280, "zqp"), (1152, "pzq"), (1152, "qpz"))


def hop(block, which):
    if which == "p":
        return lax.ppermute(block, "y", [(i, i ^ 1) for i in range(4)])
    if which == "q":
        return lax.ppermute(block, "y", [(i, 3 - i) for i in range(4)])
    if which == "z":
        return lax.ppermute(block, "zl", [(0, 1), (1, 0)])
    if which == "m":
        return lax.ppermute(block, ("zh", "zl"), [(i, 3 - i) for i in range(4)])
    if which == "h":
        return lax.ppermute(block, "zh", [(0, 1), (1, 0)])
    if which == "x":
        route = [(2 * i, 2 * ((i + 1) % 4)) for i in range(4)]
        route += [(2 * i + 1, 2 * ((i + 3) % 4) + 1) for i in range(4)]
        return lax.ppermute(block, ("x", "zh"), route)
    return lax.ppermute(block, "c", [(0, 1), (1, 0)])


AXIS_OF = {"z": 0, "q": 1, "p": 2}


def gather_rows(block, order):
    r, t, w = block.shape
    held = block.reshape(r, 1, 1, 1, t, w)
    for which in order:
        held = jnp.concatenate([held, hop(held, which)], axis=1 + AXIS_OF[which])
    return held.reshape(r, 8 * t, w)


def context_chunk(block, early, order):
    block = block[None]
    if early:
        second = hop(block, "m")
        third = hop(second, "x")
        own = gather_rows(jnp.concatenate([block, second, third], axis=0), order)
        other = hop(own, "c")
        return [(own[i], other[i]) for i in range(3)]
    first = gather_rows(block, order)[0]
    second = hop(first, "m")
    third = hop(second, "x")
    return [(part, hop(part, "c")) for part in (first, second, third)]


def update_kernel(scale, n_parts, stacked, *refs):
    cots = refs[:3]
    if stacked:
        own_ref, other_ref = refs[3:5]
        parts = [(own_ref[i], other_ref[i]) for i in range(3)]
        weight_ref = refs[5]
    else:
        parts = [(refs[3 + 2 * i][...], refs[4 + 2 * i][...]) for i in range(3)]
        weight_ref = refs[9]
    out_ref = refs[-1]
    total = weight_ref[...].astype(jnp.float32)
    for cot_ref, (own, other) in zip(cots, parts):
        half = own.shape[0]
        g = jnp.dot(cot_ref[:, :half], own, preferred_element_type=jnp.float32)
        g += jnp.dot(cot_ref[:, half:], other, preferred_element_type=jnp.float32)
        top = jnp.max(g, axis=0, keepdims=True)
        spread = top - jnp.min(g, axis=0, keepdims=True)
        code = (((top - g) * (1.0 / spread)) * 255.0).astype(jnp.bfloat16)
        low = top * (-0.25 * scale / 3.0)
        step = spread * (0.25 * scale / (3.0 * 255.0))
        total += low + code.astype(jnp.float32) * step
    out_ref[...] = total


def update(cots, parts, stacked, weight_t, out, first_column, width, tile, scale):
    rows, columns = weight_t.shape
    tokens = cots[0].shape[1]
    base = first_column // tile
    whole = pl.BlockSpec((rows, tokens), lambda j: (0, 0))
    if stacked:
        part_spec = [pl.BlockSpec((3, tokens // 2, tile), lambda j: (0, 0, j))] * 2
    else:
        part_spec = [pl.BlockSpec((tokens // 2, tile), lambda j: (0, j))] * 6
    here = pl.BlockSpec((rows, tile), lambda j: (0, base + j))
    args = [*cots, *parts, weight_t]
    specs = [whole] * 3 + part_spec + [here]
    aliases = {}
    if out is not None:
        aliases = {len(args): 0}
        args.append(out)
        specs.append(pl.BlockSpec(memory_space=pl.ANY))
    return pl.pallas_call(
        lambda *refs: update_kernel(scale, 3, stacked, *refs),
        grid=(width // tile,),
        in_specs=specs,
        out_specs=here,
        out_shape=jax.ShapeDtypeStruct((rows, columns), jnp.float32),
        input_output_aliases=aliases,
        compiler_params=pltpu.CompilerParams(
            dimension_semantics=("arbitrary",), vmem_limit_bytes=40 * 2**20
        ),
        cost_estimate=pl.CostEstimate(
            flops=3 * 2 * rows * tokens * width * 2,
            bytes_accessed=3 * tokens * width * 2 + rows * width * 6,
            transcendentals=0,
        ),
    )(*args)


def body(context, cotangent, weight):
    tokens, width = context.shape
    scale = width ** (-0.5)
    y, zl, c = (lax.axis_index(name) for name in LOCAL)
    weight_t = weight.T
    block = weight_t.shape[0]
    half = width // 2

    sizes = jnp.stack([
        jnp.max(jnp.abs(cotangent)).astype(jnp.float32),
        jnp.max(jnp.abs(weight_t)).astype(jnp.float32),
    ])
    sizes = jnp.maximum(lax.pmax(sizes, LOCAL), 2.0**-120)
    cot_size, weight_size = sizes[0], sizes[1]

    weight_own = lax.dynamic_slice_in_dim(weight_t, c * half, half, axis=1)
    weight_other = hop(lax.dynamic_slice_in_dim(weight_t, (1 - c) * half, half, axis=1), "c")

    blocks = lax.all_to_all(
        cotangent.reshape(tokens, 16, block).transpose(1, 0, 2), LOCAL, split_axis=0, concat_axis=0, tiled=True
    )
    picked = [
        lax.dynamic_index_in_dim(blocks, (y ^ (p ^ (3 * q))) * 4 + (zl ^ jz) * 2 + (c ^ jc), 0, keepdims=False)
        for jc in range(2) for jz in range(2) for q in range(2) for p in range(2)
    ]
    cot = jnp.concatenate(picked, axis=0)
    rows = cot.shape[0]
    cot_other = hop(cot, "c")
    cot_other = jnp.concatenate([cot_other[rows // 2:], cot_other[: rows // 2]], axis=0)
    cot_t = cot.T
    quarter = rows // 4
    second_t = hop(cot_t, "h")
    second_t = jnp.concatenate(
        [second_t[:, i * quarter:(i + 1) * quarter] for i in (1, 0, 3, 2)], axis=1
    )
    third_t = hop(second_t, "x")
    cots = (cot_t, second_t, third_t)

    finished = []
    start = 0
    for columns, order in SUMS:
        cols = slice(start, start + columns)
        start += columns
        part = jnp.dot(cot, weight_own[:, cols], preferred_element_type=jnp.float32)
        part += jnp.dot(cot_other, weight_other[:, cols], preferred_element_type=jnp.float32)
        held = ((part * (1.0 / cot_size)) * (1.0 / weight_size)).astype(jnp.float16)
        held = held.reshape(2, 2, 2, 2, tokens, columns)
        for which in order:
            axis = 1 + AXIS_OF[which]
            keep, send = lax.index_in_dim(held, 0, axis), lax.index_in_dim(held, 1, axis)
            held = keep.astype(jnp.float32) + hop(send.astype(jnp.float16), which).astype(jnp.float32)
        finished.append(held.reshape(2, tokens, columns))
    summed = jnp.concatenate(finished, axis=2) * (cot_size * scale) * weight_size
    summed = summed.astype(jnp.bfloat16)
    arrived = hop(summed[1], "c")
    input_grad = jnp.where(
        c == 0,
        jnp.concatenate([summed[0], arrived], axis=1),
        jnp.concatenate([arrived, summed[0]], axis=1),
    )

    out = None
    start = 0
    for columns, early, order in PLAN:
        parts = context_chunk(context[:, start:start + columns], early, order)
        if early:
            pass
        flat = [half_part for pair in parts for half_part in pair]
        out = update(cots, flat, False, weight_t, out, start, columns, 512, scale)
        start += columns
    return input_grad, out.T[None]


def solution(mesh):
    sub = Mesh(mesh.devices.reshape(SIZES), AXES)
    tokens = P(AXES, None)
    return jax.shard_map(
        body,
        mesh=sub,
        in_specs=(tokens, tokens, P(None, LOCAL)),
        out_specs=(tokens, P(("x", "zh"), None, LOCAL)),
        check_vma=False,
    )
```

time: 701 us -> 485 us (0.69); the launches traced: 701 us -> 476 us
  waiting for transfers between devices: 583 us -> 188 us
  starting transfers between devices: 14 us -> 94.3 us
  local copies, waits for them, and re-layouts: 2.97 us -> 61.8 us
  Pallas kernels: 0 us -> 54.5 us
  between operations: 14.1 us -> 3.79 us
  matrix products: 30.5 us -> 20.6 us
    ppermute x6 -> x66, waiting for transfers between devices: 418 us -> 188 us  [the longest x10 48.8 us: hop(): return lax.ppermute(block, 'y', [(i, 3 - i) for i in range(4)])]
    reduce_scatter x1 -> x0, waiting for transfers between devices: 118 us -> none  [body(): lax.psum_scatter(jnp.dot(rows, weight.T, preferred_element_type=jnp.float...]
    ppermute x6 -> x66, starting transfers between devices: 13.9 us -> 86.9 us  [the longest x20 38.7 us: hop(): return lax.ppermute(block, 'c', [(0, 1), (1, 0)])]
    pallas_call x0 -> x7, Pallas kernels: none -> 54.5 us  [update(): pl.pallas_call(lambda *refs: update_kernel(scale, 3, stacked, *refs), gri...]
    all_gather x1 -> x0, waiting for transfers between devices: 45.8 us -> none  [body(): lax.all_gather(context, 'local', axis=0, tiled=True)]
    dynamic_slice x0 -> x18, local copies, waits for them, and re-layouts: none -> 29.7 us  [the longest x17 23.6 us: body(): lax.dynamic_index_in_dim(blocks, (y ^ (p ^ 3 * q)) * 4 + (zl ^ jz) * 2 +...]
    all_to_all x1 -> x0, blocking collectives: 29.5 us -> none  [body(): lax.all_to_all(cotangent, 'local', split_axis=1, concat_axis=0, tiled=True)]
    pmax x0 -> x1, blocking collectives: none -> 28.2 us  [body(): sizes = jnp.maximum(lax.pmax(sizes, LOCAL), 2.0 ** (-120))]
  transfers between devices with their start and end apart: 8 -> 67, of which waited for: 5 -> 24; matrix products, arithmetic and copies ran while one was open for 8% -> 21% of each run, Pallas kernels for 0% -> 8%
where the time goes in v1:
time: 485 us; the launch traced here: 476 us
  waiting for transfers between devices  188 us (39%)
  starting transfers between devices  94.3 us (19%)
  local copies, waits for them, and re-layouts  61.8 us (13%)
  Pallas kernels  54.5 us (11%)
  blocking collectives  28.2 us (6%)
  other arithmetic  24.8 us (5%)
  matrix products  20.6 us (4%)
    pallas_call x7, Pallas kernels, update(): pl.pallas_call(lambda *refs: update_kernel(scale, 3, stacked, *refs), gri...  54.5 us
    ppermute x10, waiting for transfers between devices, hop(): return lax.ppermute(block, 'y', [(i, 3 - i) for i in range(4)])  48.8 us
    ppermute x8, waiting for transfers between devices, hop(): return lax.ppermute(block, ('x', 'zh'), route)  39 us
    ppermute x20, starting transfers between devices, hop(): return lax.ppermute(block, 'c', [(0, 1), (1, 0)])  38.7 us
    ppermute x7, waiting for transfers between devices, hop(): return lax.ppermute(block, ('zh', 'zl'), [(i, 3 - i) for i in range(4)])  37 us
    ppermute x10, waiting for transfers between devices, hop(): return lax.ppermute(block, 'zl', [(0, 1), (1, 0)])  33.6 us
    pmax x1, blocking collectives, body(): sizes = jnp.maximum(lax.pmax(sizes, LOCAL), 2.0 ** (-120))  28.2 us
    dynamic_slice x17, local copies, waits for them, and re-layouts, body(): lax.dynamic_index_in_dim(blocks, (y ^ (p ^ 3 * q)) * 4 + (zl ^ jz) * 2 +...  23.6 us
  transfers between devices with their start and end apart: 67, of which 24 were waited for; matrix products, arithmetic and copies ran while one was open for 21% of the time, Pallas kernels for 8%

profile of v1, /device:TPU:1, one launch (start us, length us, event | category | flops | bytes accessed | tf_op | source)
XLA Modules:
  0.0 476.2 jit_solution(16587469587743059206)
XLA Ops:
  0.6 2.4 reshape.53
  4.5 7.5 %all-to-all-start = ((bf16[16,64,448]{2,1,0:T(8,128)(2,1)}), bf16[16,64,448]{2,1,0:T(8,128)(2,1)S(1)}, u32[]{:S(2)}, u32[]{:S(2)}) async-start(bf16[16,64,448]{2,1,0:T(8,128)(2,1)} %copy.44), calls=%async_computation | async-start | bytes 2097152 | tf_op jit(solution)/shard_map/all_to_all | solution.py:144
  14.9 2.6 collective-permute-start.42
  17.5 3.3 collective-permute-start.28
  21.5 4.3 abs_reduce_fusion
  27.1 28.2 %pmax.7 = f32[2]{0:T(128)S(1)} all-reduce(f32[2]{0:T(128)S(1)} %maximum_convert_fusion), channel_id=1, replica_groups=mesh['x'=4,'zh'=2,'y'=4,'zl'=2,'c'=2] {'y','zl','c'}, use_global_device_ids=true, to_apply=%region_2.0 | all-reduce | flops 2 | bytes 16 | tf_op jit(solution)/shard_map/pmax | solution.py:138
  55.3 6.1 %dynamic-slice_bitcast_fusion = (bf16[448,3584]{1,0:T(8,128)(2,1)}, bf16[448,3584]{1,0:T(8,128)(2,1)}) fusion(bf16[7168,448]{0,1:T(8,128)(2,1)} %param.5, s32[]{:T(128)S(6)} %select_n.81, s32[]{:T(128)S(6)} %select_n.80), kind=kLoop, calls=%fused_computation.10 | loop fusion | bytes 12845064 | tf_op jit(solution)/shard_map/dynamic_slice | solution.py:142
  64.4 2.7 collective-permute-start.59
  72.7 2.6 collective-permute-start.35
  77.5 3.5 collective-permute-done.51
  84.3 2.4 collective-permute-done.35
  92.9 2.3 collective-permute-start.17
  97.2 1.6 copy.54
  102.0 1.6 copy.57
  105.2 1.6 copy.59
  106.8 1.6 copy.60
  118.8 2.8 concatenate.87
  121.6 5.3 %fusion.9 = f32[1024,1280]{1,0:T(8,128)} fusion(bf16[1024,448]{0,1:T(8,128)(2,1)S(1)} %concatenate.87, bf16[448,3584]{1,0:T(8,128)(2,1)} %get-tuple-element.3), kind=kOutput, calls=%fused_computation.29 | convolution fusion | flops 1174405120 | bytes 7307264 | tf_op jit(solution)/shard_map/dot_general | solution.py:169
  126.9 3.8 fusion.15
  130.7 8.3 %collective-permute-start.1 = (bf16[448,3584]{1,0:T(8,128)(2,1)S(1)}, bf16[448,3584]{1,0:T(8,128)(2,1)S(1)}, u32[]{:S(2)}, u32[]{:S(2)}) collective-permute-start(bf16[448,3584]{1,0:T(8,128)(2,1)S(1)} %copy-done.12), channel_id=1, source_target_pairs={{0,1},{1,0},{2,3},{3,2},{4,5},{5,4},{6,7},{7,6},{8,9},{9,8},{10,11... | collective-permute-start | bytes 9633800 | tf_op jit(solution)/shard_map/ppermute | solution.py:39
  145.5 8.3 %collective-permute-done.36 = bf16[1,1,2,2,64,1024]{5,4,3,2,1,0:T(8,128)(2,1)S(1)} collective-permute-done((bf16[1,1,2,2,64,1024]{5,4,3,2,1,0:T(8,128)(2,1)S(1)}, bf16[1,1,2,2,64,1024]{5,4,3,2,1,0:T(8,128)(2,1)S(1)}, u32[]{:S(2)}, u32[]{:S(2)}) %collective-permute-start.36) | collective-permute-done | bytes 524320 | tf_op jit(solution)/shard_map/ppermute | solution.py:30
  156.2 8.9 %collective-permute-done.22 = bf16[1,1,2,2,64,1024]{5,4,3,2,1,0:T(8,128)(2,1)S(1)} collective-permute-done((bf16[1,1,2,2,64,1024]{5,4,3,2,1,0:T(8,128)(2,1)S(1)}, bf16[1,1,2,2,64,1024]{5,4,3,2,1,0:T(8,128)(2,1)S(1)}, u32[]{:S(2)}, u32[]{:S(2)}) %collective-permute-start.22) | collective-permute-done | bytes 524320 | tf_op jit(solution)/shard_map/ppermute | solution.py:30
  169.1 16.8 %collective-permute-done.12 = bf16[448,1024]{1,0:T(8,128)(2,1)S(1)} collective-permute-done((bf16[448,1024]{1,0:T(8,128)(2,1)S(1)}, bf16[448,1024]{1,0:T(8,128)(2,1)S(1)}, u32[]{:S(2)}, u32[]{:S(2)}) %collective-permute-start.12) | collective-permute-done | bytes 917536 | tf_op jit(solution)/shard_map/ppermute | solution.py:34
  191.6 2.1 copy.68
  194.3 2.2 copy.67
  199.0 4.2 multiply_convert_fusion
  203.2 1.6 fusion.25
  206.1 4.8 %collective-permute-done.62.refs_5_ = bf16[512,1024]{1,0:T(8,128)(2,1)S(1)} collective-permute-done((bf16[512,1024]{1,0:T(8,128)(2,1)S(1)}, bf16[512,1024]{1,0:T(8,128)(2,1)S(1)}, u32[]{:S(2)}, u32[]{:S(2)}) %collective-permute-start.62) | collective-permute-done | bytes 1048608 | tf_op jit(solution)/shard_map/ppermute | solution.py:32
  213.0 20.5 %collective-permute-done.54.refs_5_ = bf16[512,1024]{1,0:T(8,128)(2,1)S(1)} collective-permute-done((bf16[512,1024]{1,0:T(8,128)(2,1)S(1)}, bf16[512,1024]{1,0:T(8,128)(2,1)S(1)}, u32[]{:S(2)}, u32[]{:S(2)}) %collective-permute-start.54) | collective-permute-done | bytes 1048608 | tf_op jit(solution)/shard_map/ppermute | solution.py:32
  234.2 4.0 fusion.4
  241.0 3.4 collective-permute-start.63
  244.4 11.6 %collective-permute-done.46.refs_5_ = bf16[512,1024]{1,0:T(8,128)(2,1)} collective-permute-done((bf16[512,1024]{1,0:T(8,128)(2,1)S(1)}, bf16[512,1024]{1,0:T(8,128)(2,1)}, u32[]{:S(2)}, u32[]{:S(2)}) %collective-permute-start.46) | collective-permute-done | bytes 1048608 | tf_op jit(solution)/shard_map/ppermute | solution.py:32
  256.0 1.8 collective-permute-start.55
  258.6 2.8 collective-permute-start.65
  261.4 15.3 %collective-permute-done.56.refs_7_ = bf16[512,1024]{1,0:T(8,128)(2,1)S(1)} collective-permute-done((bf16[512,1024]{1,0:T(8,128)(2,1)S(1)}, bf16[512,1024]{1,0:T(8,128)(2,1)S(1)}, u32[]{:S(2)}, u32[]{:S(2)}) %collective-permute-start.56) | collective-permute-done | bytes 1048608 | tf_op jit(solution)/shard_map/ppermute | solution.py:38
  276.7 7.1 %collective-permute-start.57 = (bf16[512,1024]{1,0:T(8,128)(2,1)S(1)}, bf16[512,1024]{1,0:T(8,128)(2,1)S(1)}, u32[]{:S(2)}, u32[]{:S(2)}) collective-permute-start(bf16[512,1024]{1,0:T(8,128)(2,1)S(1)} %collective-permute-done.56.refs_7_), channel_id=1, source_target_pairs={{0,1},{1,0},{2,3},{3,2},{4,5},{5,4},{6,7},{7,6},{8,9},{9,8},{10,11... | collective-permute-start | bytes 3145736 | tf_op jit(solution)/shard_map/ppermute | solution.py:39
  283.8 1.7 fusion.5
  289.3 10.0 %collective-permute-done.48.refs_7_ = bf16[512,1024]{1,0:T(8,128)(2,1)} collective-permute-done((bf16[512,1024]{1,0:T(8,128)(2,1)}, bf16[512,1024]{1,0:T(8,128)(2,1)}, u32[]{:S(2)}, u32[]{:S(2)}) %collective-permute-start.48) | collective-permute-done | bytes 1048608 | tf_op jit(solution)/shard_map/ppermute | solution.py:38
  299.3 3.8 collective-permute-start.47
  304.5 8.0 %shard_map.50.refs_10_ = f32[448,7168]{1,0:T(8,128)} custom-call(bf16[448,1024]{1,0:T(8,128)(2,1)S(1)} %bitcast.92, bf16[448,1024]{1,0:T(8,128)(2,1)S(1)} %pad_maximum_fusion.10.refs_1_, bf16[448,1024]{1,0:T(8,128)(2,1)S(1)} %collective-permute-done.13.refs_2_, bf16[512,1024]{1,0:T(8,128)(2,1)S(1)} %bitcast.101, ...), custom_call_target="tpu_custom_call" | custom-call | flops 5637144576 | bytes 9043968 | tf_op jit(solution)/shard_map/pallas_call | solution.py:108
  315.0 7.6 %shard_map.51.refs_10_ = f32[448,7168]{1,0:T(8,128)} custom-call(bf16[448,1024]{1,0:T(8,128)(2,1)S(1)} %bitcast.93, bf16[448,1024]{1,0:T(8,128)(2,1)S(1)} %pad_maximum_fusion.10.refs_1_, bf16[448,1024]{1,0:T(8,128)(2,1)S(1)} %collective-permute-done.13.refs_2_, bf16[512,1024]{1,0:T(8,128)(2,1)S(1)} %bitcast.113, ...), custom_call_target="tpu_custom_call", output_to_operand_aliasing={{}: (10, {})} | custom-call | flops 5637144576 | bytes 9043968 | tf_op jit(solution)/shard_map/pallas_call | solution.py:108
  323.9 8.3 %shard_map.52.refs_10_ = f32[448,7168]{1,0:T(8,128)} custom-call(bf16[448,1024]{1,0:T(8,128)(2,1)S(1)} %bitcast.94, bf16[448,1024]{1,0:T(8,128)(2,1)S(1)} %pad_maximum_fusion.10.refs_1_, bf16[448,1024]{1,0:T(8,128)(2,1)S(1)} %collective-permute-done.13.refs_2_, bf16[512,1024]{1,0:T(8,128)(2,1)S(1)} %bitcast.110, ...), custom_call_target="tpu_custom_call", output_to_operand_aliasing={{}: (10, {})} | custom-call | flops 5637144576 | bytes 9043968 | tf_op jit(solution)/shard_map/pallas_call | solution.py:108
  332.3 2.4 collective-permute-start.8
  334.7 1.6 convert_add_fusion.2
  336.4 24.0 %collective-permute-done.8 = f16[2,2,1,2,64,1152]{5,4,0,3,2,1:T(8,128)(2,1)S(1)} collective-permute-done((f16[2,2,1,2,64,1152]{5,4,0,3,2,1:T(8,128)(2,1)}, f16[2,2,1,2,64,1152]{5,4,0,3,2,1:T(8,128)(2,1)S(1)}, u32[]{:S(2)}, u32[]{:S(2)}) %collective-permute-start.8) | collective-permute-done | bytes 1179680 | tf_op jit(solution)/shard_map/ppermute | solution.py:28
  360.4 1.7 collective-permute-start.6
  363.8 10.1 %collective-permute-done.6 = f16[2,1,2,1,64,1152]{5,4,0,3,2,1:T(8,128)(2,1)S(1)} collective-permute-done((f16[2,1,2,1,64,1152]{5,4,0,3,2,1:T(8,128)(2,1)S(1)}, f16[2,1,2,1,64,1152]{5,4,0,3,2,1:T(8,128)(2,1)S(1)}, u32[]{:S(2)}, u32[]{:S(2)}) %collective-permute-start.6) | collective-permute-done | bytes 589856 | tf_op jit(solution)/shard_map/ppermute | solution.py:30
  373.9 2.5 collective-permute-start.33
  376.5 3.1 collective-permute-start.3
  379.8 13.2 %collective-permute-done.3 = f16[2,1,1,2,64,1280]{5,4,0,3,2,1:T(8,128)(2,1)S(1)} collective-permute-done((f16[2,1,1,2,64,1280]{5,4,0,3,2,1:T(8,128)(2,1)S(1)}, f16[2,1,1,2,64,1280]{5,4,0,3,2,1:T(8,128)(2,1)S(1)}, u32[]{:S(2)}, u32[]{:S(2)}) %collective-permute-start.3) | collective-permute-done | bytes 655392 | tf_op jit(solution)/shard_map/ppermute | solution.py:28
  393.0 2.7 collective-permute-start.7
  395.8 4.5 collective-permute-done.7
  400.4 3.4 collective-permute-start.10
  403.8 5.1 %collective-permute-done.10 = f16[2,1,1,1,64,1152]{5,4,0,3,2,1:T(8,128)(2,1)S(1)} collective-permute-done((f16[2,1,1,1,64,1152]{5,4,0,3,2,1:T(8,128)(2,1)S(1)}, f16[2,1,1,1,64,1152]{5,4,0,3,2,1:T(8,128)(2,1)S(1)}, u32[]{:S(2)}, u32[]{:S(2)}) %collective-permute-start.10) | collective-permute-done | bytes 294944 | tf_op jit(solution)/shard_map/ppermute | solution.py:30
  409.2 6.4 %collective-permute-done.4 = f16[2,1,1,1,64,1280]{5,4,0,3,2,1:T(8,128)(2,1)S(1)} collective-permute-done((f16[2,1,1,1,64,1280]{5,4,0,3,2,1:T(8,128)(2,1)S(1)}, f16[2,1,1,1,64,1280]{5,4,0,3,2,1:T(8,128)(2,1)S(1)}, u32[]{:S(2)}, u32[]{:S(2)}) %collective-permute-start.4) | collective-permute-done | bytes 327712 | tf_op jit(solution)/shard_map/ppermute | solution.py:26
  415.6 3.7 collective-permute-start.19
  420.9 5.0 %collective-permute-done.39.refs_6_ = bf16[512,1024]{1,0:T(8,128)(2,1)S(1)} collective-permute-done((bf16[512,1024]{1,0:T(8,128)(2,1)S(1)}, bf16[512,1024]{1,0:T(8,128)(2,1)S(1)}, u32[]{:S(2)}, u32[]{:S(2)}) %collective-permute-start.39) | collective-permute-done | bytes 1048608 | tf_op jit(solution)/shard_map/ppermute | solution.py:39
  427.9 7.6 %shard_map.53.refs_10_ = f32[448,7168]{1,0:T(8,128)} custom-call(bf16[448,1024]{1,0:T(8,128)(2,1)S(1)} %bitcast.95, bf16[448,1024]{1,0:T(8,128)(2,1)S(1)} %pad_maximum_fusion.10.refs_1_, bf16[448,1024]{1,0:T(8,128)(2,1)S(1)} %collective-permute-done.13.refs_2_, bf16[512,1024]{1,0:T(8,128)(2,1)S(1)} %bitcast.107, ...), custom_call_target="tpu_custom_call", output_to_operand_aliasing={{}: (10, {})} | custom-call | flops 5637144576 | bytes 9043968 | tf_op jit(solution)/shard_map/pallas_call | solution.py:108
  435.5 11.2 %collective-permute-done.26.refs_7_ = bf16[512,1024]{1,0:T(8,128)(2,1)S(1)} collective-permute-done((bf16[512,1024]{1,0:T(8,128)(2,1)S(1)}, bf16[512,1024]{1,0:T(8,128)(2,1)S(1)}, u32[]{:S(2)}, u32[]{:S(2)}) %collective-permute-start.26) | collective-permute-done | bytes 1048608 | tf_op jit(solution)/shard_map/ppermute | solution.py:38
  448.7 2.2 slice_bitcast_fusion
  450.9 2.2 slice_bitcast_fusion.3
  453.1 7.7 %shard_map.54.refs_10_ = f32[448,7168]{1,0:T(8,128)} custom-call(bf16[448,1024]{1,0:T(8,128)(2,1)S(1)} %bitcast.96, bf16[448,1024]{1,0:T(8,128)(2,1)S(1)} %pad_maximum_fusion.10.refs_1_, bf16[448,1024]{1,0:T(8,128)(2,1)S(1)} %collective-permute-done.13.refs_2_, bf16[512,1024]{1,0:T(8,128)(2,1)S(1)} %bitcast.119, ...), custom_call_target="tpu_custom_call", output_to_operand_aliasing={{}: (10, {})} | custom-call | flops 5637144576 | bytes 9043968 | tf_op jit(solution)/shard_map/pallas_call | solution.py:108
  460.8 7.7 %shard_map.55.refs_10_ = f32[448,7168]{1,0:T(8,128)} custom-call(bf16[448,1024]{1,0:T(8,128)(2,1)S(1)} %bitcast.97, bf16[448,1024]{1,0:T(8,128)(2,1)S(1)} %pad_maximum_fusion.10.refs_1_, bf16[448,1024]{1,0:T(8,128)(2,1)S(1)} %collective-permute-done.13.refs_2_, bf16[512,1024]{1,0:T(8,128)(2,1)S(1)} %bitcast.104, ...), custom_call_target="tpu_custom_call", output_to_operand_aliasing={{}: (10, {})} | custom-call | flops 5637144576 | bytes 9043968 | tf_op jit(solution)/shard_map/pallas_call | solution.py:108
  468.4 7.6 %shard_map.56 = f32[448,7168]{1,0:T(8,128)} custom-call(bf16[448,1024]{1,0:T(8,128)(2,1)S(1)} %bitcast.98, bf16[448,1024]{1,0:T(8,128)(2,1)S(1)} %pad_maximum_fusion.10.refs_1_, bf16[448,1024]{1,0:T(8,128)(2,1)S(1)} %collective-permute-done.13.refs_2_, bf16[512,1024]{1,0:T(8,128)(2,1)S(1)} %bitcast.116, ...), custom_call_target="tpu_custom_call", output_to_operand_aliasing={{}: (10, {})} | custom-call | flops 5637144576 | bytes 9043968 | tf_op jit(solution)/shard_map/pallas_call | solution.py:108
  (261 shorter events, 87.7 us)
Async XLA Ops:
  4.5 90.6 %all-to-all-start = ((bf16[16,64,448]{2,1,0:T(8,128)(2,1)}), bf16[16,64,448]{2,1,0:T(8,128)(2,1)S(1)}, u32[]{:S(2)}, u32[]{:S(2)}) async-start(bf16[16,64,448]{2,1,0:T(8,128)(2,1)} %copy.44), calls=%async_computation | async-start | bytes 2097152 | tf_op jit(solution)/shard_map/all_to_all | solution.py:144
  13.4 50.7 %collective-permute-start.58 = (bf16[1,1,1,1,64,1024]{5,4,3,2,1,0:T(8,128)(2,1)S(1)}, bf16[1,1,1,1,64,1024]{5,4,3,2,1,0:T(8,128)(2,1)S(1)}, u32[]{:S(2)}, u32[]{:S(2)}) collective-permute-start(bf16[1,1,1,1,64,1024]{5,4,3,2,1,0:T(8,128)(2,1)S(1)} %get-tuple-element.38), channel_id=1, source_target_pairs={{0,4},{4,0},{8,12},{12,8},{1,5},{5,1},{9,13},{13,9},{2,6},{6,2},{1... | collective-permute-start | bytes 393224 | tf_op jit(solution)/shard_map/ppermute | solution.py:26
  14.8 49.4 %collective-permute-start.50 = (bf16[1,1,1,1,64,1024]{5,4,3,2,1,0:T(8,128)(2,1)S(1)}, bf16[1,1,1,1,64,1024]{5,4,3,2,1,0:T(8,128)(2,1)S(1)}, u32[]{:S(2)}, u32[]{:S(2)}) collective-permute-start(bf16[1,1,1,1,64,1024]{5,4,3,2,1,0:T(8,128)(2,1)S(1)} %get-tuple-element.44), channel_id=1, source_target_pairs={{0,4},{4,0},{8,12},{12,8},{1,5},{5,1},{9,13},{13,9},{2,6},{6,2},{1... | collective-permute-start | bytes 393224 | tf_op jit(solution)/shard_map/ppermute | solution.py:26
  14.9 49.4 %collective-permute-start.42 = (bf16[1,1,1,1,64,1024]{5,4,3,2,1,0:T(8,128)(2,1)S(1)}, bf16[1,1,1,1,64,1024]{5,4,3,2,1,0:T(8,128)(2,1)S(1)}, u32[]{:S(2)}, u32[]{:S(2)}) collective-permute-start(bf16[1,1,1,1,64,1024]{5,4,3,2,1,0:T(8,128)(2,1)S(1)} %get-tuple-element.39), channel_id=1, source_target_pairs={{0,12},{4,8},{8,4},{12,0},{1,13},{5,9},{9,5},{13,1},{2,14},{6,10},... | collective-permute-start | bytes 393224 | tf_op jit(solution)/shard_map/ppermute | solution.py:28
  17.5 49.7 %collective-permute-start.34 = (bf16[1,1,1,1,64,1024]{5,4,3,2,1,0:T(8,128)(2,1)S(1)}, bf16[1,1,1,1,64,1024]{5,4,3,2,1,0:T(8,128)(2,1)S(1)}, u32[]{:S(2)}, u32[]{:S(2)}) collective-permute-start(bf16[1,1,1,1,64,1024]{5,4,3,2,1,0:T(8,128)(2,1)S(1)} %get-tuple-element.40), channel_id=1, source_target_pairs={{0,4},{4,0},{8,12},{12,8},{1,5},{5,1},{9,13},{13,9},{2,6},{6,2},{1... | collective-permute-start | bytes 393224 | tf_op jit(solution)/shard_map/ppermute | solution.py:26
  17.5 49.8 %collective-permute-start.28 = (bf16[1,64,1024]{2,1,0:T(8,128)(2,1)S(1)}, bf16[1,64,1024]{2,1,0:T(8,128)(2,1)S(1)}, u32[]{:S(2)}, u32[]{:S(2)}) collective-permute-start(bf16[1,64,1024]{2,1,0:T(8,128)(2,1)S(1)} %get-tuple-element.41), channel_id=1, source_target_pairs={{0,18},{2,16},{16,2},{18,0},{1,19},{3,17},{17,3},{19,1},{4,22},{6,... | collective-permute-start | bytes 393224 | tf_op jit(solution)/shard_map/ppermute | solution.py:32
  64.4 12.0 %collective-permute-start.59 = (bf16[1,1,1,2,64,1024]{5,4,3,2,1,0:T(8,128)(2,1)S(1)}, bf16[1,1,1,2,64,1024]{5,4,3,2,1,0:T(8,128)(2,1)S(1)}, u32[]{:S(2)}, u32[]{:S(2)}) collective-permute-start(bf16[1,1,1,2,64,1024]{5,4,3,2,1,0:T(8,128)(2,1)S(1)} %pad_maximum_fusion.25), channel_id=1, source_target_pairs={{0,12},{4,8},{8,4},{12,0},{1,13},{5,9},{9,5},{13,1},{2,14},{6,10},... | collective-permute-start | bytes 786440 | tf_op jit(solution)/shard_map/ppermute | solution.py:28
  67.2 13.8 %collective-permute-start.51 = (bf16[1,1,1,2,64,1024]{5,4,3,2,1,0:T(8,128)(2,1)S(1)}, bf16[1,1,1,2,64,1024]{5,4,3,2,1,0:T(8,128)(2,1)S(1)}, u32[]{:S(2)}, u32[]{:S(2)}) collective-permute-start(bf16[1,1,1,2,64,1024]{5,4,3,2,1,0:T(8,128)(2,1)S(1)} %pad_maximum_fusion.24), channel_id=1, source_target_pairs={{0,12},{4,8},{8,4},{12,0},{1,13},{5,9},{9,5},{13,1},{2,14},{6,10},... | collective-permute-start | bytes 786440 | tf_op jit(solution)/shard_map/ppermute | solution.py:28
  69.8 12.2 %collective-permute-start.43 = (bf16[1,1,2,1,64,1024]{5,4,3,2,1,0:T(8,128)(2,1)S(1)}, bf16[1,1,2,1,64,1024]{5,4,3,2,1,0:T(8,128)(2,1)S(1)}, u32[]{:S(2)}, u32[]{:S(2)}) collective-permute-start(bf16[1,1,2,1,64,1024]{5,4,3,2,1,0:T(8,128)(2,1)S(1)} %pad_maximum_fusion.23), channel_id=1, source_target_pairs={{0,4},{4,0},{8,12},{12,8},{1,5},{5,1},{9,13},{13,9},{2,6},{6,2},{1... | collective-permute-start | bytes 786440 | tf_op jit(solution)/shard_map/ppermute | solution.py:26
  69.9 6.4 %collective-permute-start.15 = (bf16[1,64,1024]{2,1,0:T(8,128)(2,1)S(1)}, bf16[1,64,1024]{2,1,0:T(8,128)(2,1)S(1)}, u32[]{:S(2)}, u32[]{:S(2)}) collective-permute-start(bf16[1,64,1024]{2,1,0:T(8,128)(2,1)S(1)} %collective-permute-done.14), channel_id=1, source_target_pairs={{0,32},{32,64},{64,96},{96,0},{16,112},{48,16},{80,48},{112,80},{1... | collective-permute-start | bytes 393224 | tf_op jit(solution)/shard_map/ppermute | solution.py:38
  72.7 14.0 %collective-permute-start.35 = (bf16[1,1,1,2,64,1024]{5,4,3,2,1,0:T(8,128)(2,1)S(1)}, bf16[1,1,1,2,64,1024]{5,4,3,2,1,0:T(8,128)(2,1)S(1)}, u32[]{:S(2)}, u32[]{:S(2)}) collective-permute-start(bf16[1,1,1,2,64,1024]{5,4,3,2,1,0:T(8,128)(2,1)S(1)} %pad_maximum_fusion.22), channel_id=1, source_target_pairs={{0,12},{4,8},{8,4},{12,0},{1,13},{5,9},{9,5},{13,1},{2,14},{6,10},... | collective-permute-start | bytes 786440 | tf_op jit(solution)/shard_map/ppermute | solution.py:28
  76.4 11.2 %collective-permute-start.21 = (bf16[1,1,2,1,64,1024]{5,4,3,2,1,0:T(8,128)(2,1)S(1)}, bf16[1,1,2,1,64,1024]{5,4,3,2,1,0:T(8,128)(2,1)S(1)}, u32[]{:S(2)}, u32[]{:S(2)}) collective-permute-start(bf16[1,1,2,1,64,1024]{5,4,3,2,1,0:T(8,128)(2,1)S(1)} %pad_maximum_fusion.21), channel_id=1, source_target_pairs={{0,4},{4,0},{8,12},{12,8},{1,5},{5,1},{9,13},{13,9},{2,6},{6,2},{1... | collective-permute-start | bytes 786440 | tf_op jit(solution)/shard_map/ppermute | solution.py:26
  76.4 13.4 %collective-permute-start.30 = (bf16[3,1,1,1,64,1024]{5,4,0,3,2,1:T(8,128)(2,1)S(1)}, bf16[3,1,1,1,64,1024]{5,4,0,3,2,1:T(8,128)(2,1)S(1)}, u32[]{:S(2)}, u32[]{:S(2)}) collective-permute-start(bf16[3,1,1,1,64,1024]{5,4,0,3,2,1:T(8,128)(2,1)S(1)} %maximum_bitcast_fusion.1), channel_id=1, source_target_pairs={{0,2},{2,0},{1,3},{3,1},{4,6},{6,4},{5,7},{7,5},{8,10},{10,8},{9,1... | collective-permute-start | bytes 1179656 | tf_op jit(solution)/shard_map/ppermute | solution.py:30
  81.0 10.9 %collective-permute-start.16 = (bf16[3,1,1,1,64,1024]{5,4,0,3,2,1:T(8,128)(2,1)S(1)}, bf16[3,1,1,1,64,1024]{5,4,0,3,2,1:T(8,128)(2,1)S(1)}, u32[]{:S(2)}, u32[]{:S(2)}) collective-permute-start(bf16[3,1,1,1,64,1024]{5,4,0,3,2,1:T(8,128)(2,1)S(1)} %maximum_bitcast_fusion), channel_id=1, source_target_pairs={{0,2},{2,0},{1,3},{3,1},{4,6},{6,4},{5,7},{7,5},{8,10},{10,8},{9,1... | collective-permute-start | bytes 1179656 | tf_op jit(solution)/shard_map/ppermute | solution.py:30
  82.0 58.3 %collective-permute-start.60 = (bf16[1,1,2,2,64,1024]{5,4,3,2,1,0:T(8,128)(2,1)}, bf16[1,1,2,2,64,1024]{5,4,3,2,1,0:T(8,128)(2,1)}, u32[]{:S(2)}, u32[]{:S(2)}) collective-permute-start(bf16[1,1,2,2,64,1024]{5,4,3,2,1,0:T(8,128)(2,1)} %pad_maximum_fusion.17), channel_id=1, source_target_pairs={{0,2},{2,0},{1,3},{3,1},{4,6},{6,4},{5,7},{7,5},{8,10},{10,8},{9,1... | collective-permute-start | bytes 1572872 | tf_op jit(solution)/shard_map/ppermute | solution.py:30
  86.7 53.8 %collective-permute-start.52 = (bf16[1,1,2,2,64,1024]{5,4,3,2,1,0:T(8,128)(2,1)}, bf16[1,1,2,2,64,1024]{5,4,3,2,1,0:T(8,128)(2,1)}, u32[]{:S(2)}, u32[]{:S(2)}) collective-permute-start(bf16[1,1,2,2,64,1024]{5,4,3,2,1,0:T(8,128)(2,1)} %pad_maximum_fusion.16), channel_id=1, source_target_pairs={{0,2},{2,0},{1,3},{3,1},{4,6},{6,4},{5,7},{7,5},{8,10},{10,8},{9,1... | collective-permute-start | bytes 1572872 | tf_op jit(solution)/shard_map/ppermute | solution.py:30
  87.6 54.3 %collective-permute-start.44 = (bf16[1,1,2,2,64,1024]{5,4,3,2,1,0:T(8,128)(2,1)}, bf16[1,1,2,2,64,1024]{5,4,3,2,1,0:T(8,128)(2,1)}, u32[]{:S(2)}, u32[]{:S(2)}) collective-permute-start(bf16[1,1,2,2,64,1024]{5,4,3,2,1,0:T(8,128)(2,1)} %pad_maximum_fusion.15), channel_id=1, source_target_pairs={{0,2},{2,0},{1,3},{3,1},{4,6},{6,4},{5,7},{7,5},{8,10},{10,8},{9,1... | collective-permute-start | bytes 1572872 | tf_op jit(solution)/shard_map/ppermute | solution.py:30
  90.9 39.9 %collective-permute-start.31 = (bf16[3,2,1,1,64,1024]{5,4,0,3,2,1:T(8,128)(2,1)}, bf16[3,2,1,1,64,1024]{5,4,0,3,2,1:T(8,128)(2,1)}, u32[]{:S(2)}, u32[]{:S(2)}) collective-permute-start(bf16[3,2,1,1,64,1024]{5,4,0,3,2,1:T(8,128)(2,1)} %pad_maximum_fusion.12), channel_id=1, source_target_pairs={{0,12},{4,8},{8,4},{12,0},{1,13},{5,9},{9,5},{13,1},{2,14},{6,10},... | collective-permute-start | bytes 2359304 | tf_op jit(solution)/shard_map/ppermute | solution.py:28
  92.9 50.2 %collective-permute-start.17 = (bf16[3,2,1,1,64,1024]{5,4,0,3,2,1:T(8,128)(2,1)}, bf16[3,2,1,1,64,1024]{5,4,0,3,2,1:T(8,128)(2,1)S(1)}, u32[]{:S(2)}, u32[]{:S(2)}) collective-permute-start(bf16[3,2,1,1,64,1024]{5,4,0,3,2,1:T(8,128)(2,1)} %pad_maximum_fusion.11), channel_id=1, source_target_pairs={{0,4},{4,0},{8,12},{12,8},{1,5},{5,1},{9,13},{13,9},{2,6},{6,2},{1... | collective-permute-start | bytes 2359304 | tf_op jit(solution)/shard_map/ppermute | solution.py:26
  130.7 66.7 %collective-permute-start.1 = (bf16[448,3584]{1,0:T(8,128)(2,1)S(1)}, bf16[448,3584]{1,0:T(8,128)(2,1)S(1)}, u32[]{:S(2)}, u32[]{:S(2)}) collective-permute-start(bf16[448,3584]{1,0:T(8,128)(2,1)S(1)} %copy-done.12), channel_id=1, source_target_pairs={{0,1},{1,0},{2,3},{3,2},{4,5},{5,4},{6,7},{7,6},{8,9},{9,8},{10,11... | collective-permute-start | bytes 9633800 | tf_op jit(solution)/shard_map/ppermute | solution.py:39
  140.3 13.6 %collective-permute-start.36 = (bf16[1,1,2,2,64,1024]{5,4,3,2,1,0:T(8,128)(2,1)S(1)}, bf16[1,1,2,2,64,1024]{5,4,3,2,1,0:T(8,128)(2,1)S(1)}, u32[]{:S(2)}, u32[]{:S(2)}) collective-permute-start(bf16[1,1,2,2,64,1024]{5,4,3,2,1,0:T(8,128)(2,1)S(1)} %copy-done.43), channel_id=1, source_target_pairs={{0,2},{2,0},{1,3},{3,1},{4,6},{6,4},{5,7},{7,5},{8,10},{10,8},{9,1... | collective-permute-start | bytes 1572872 | tf_op jit(solution)/shard_map/ppermute | solution.py:30
  140.4 24.7 %collective-permute-start.22 = (bf16[1,1,2,2,64,1024]{5,4,3,2,1,0:T(8,128)(2,1)S(1)}, bf16[1,1,2,2,64,1024]{5,4,3,2,1,0:T(8,128)(2,1)S(1)}, u32[]{:S(2)}, u32[]{:S(2)}) collective-permute-start(bf16[1,1,2,2,64,1024]{5,4,3,2,1,0:T(8,128)(2,1)S(1)} %copy-done.42), channel_id=1, source_target_pairs={{0,2},{2,0},{1,3},{3,1},{4,6},{6,4},{5,7},{7,5},{8,10},{10,8},{9,1... | collective-permute-start | bytes 1572872 | tf_op jit(solution)/shard_map/ppermute | solution.py:30
  141.9 44.1 %collective-permute-start.12 = (bf16[448,1024]{1,0:T(8,128)(2,1)S(1)}, bf16[448,1024]{1,0:T(8,128)(2,1)S(1)}, u32[]{:S(2)}, u32[]{:S(2)}) collective-permute-start(bf16[448,1024]{1,0:T(8,128)(2,1)S(1)} %bitcast.91), channel_id=1, source_target_pairs={{0,16},{16,0},{1,17},{17,1},{2,18},{18,2},{3,19},{19,3},{4,20},{20... | collective-permute-start | bytes 2752520 | tf_op jit(solution)/shard_map/ppermute | solution.py:34
  143.1 45.5 %collective-permute-start.32 = (bf16[3,2,2,1,64,1024]{5,4,0,3,2,1:T(8,128)(2,1)S(1)}, bf16[3,2,2,1,64,1024]{5,4,0,3,2,1:T(8,128)(2,1)S(1)}, u32[]{:S(2)}, u32[]{:S(2)}) collective-permute-start(bf16[3,2,2,1,64,1024]{5,4,0,3,2,1:T(8,128)(2,1)S(1)} %pad_maximum_fusion.3), channel_id=1, source_target_pairs={{0,4},{4,0},{8,12},{12,8},{1,5},{5,1},{9,13},{13,9},{2,6},{6,2},{1... | collective-permute-start | bytes 4718600 | tf_op jit(solution)/shard_map/ppermute | solution.py:26
  153.9 39.8 %collective-permute-start.18 = (bf16[3,2,1,2,64,1024]{5,4,0,3,2,1:T(8,128)(2,1)S(1)}, bf16[3,2,1,2,64,1024]{5,4,0,3,2,1:T(8,128)(2,1)S(1)}, u32[]{:S(2)}, u32[]{:S(2)}) collective-permute-start(bf16[3,2,1,2,64,1024]{5,4,0,3,2,1:T(8,128)(2,1)S(1)} %pad_maximum_fusion.2), channel_id=1, source_target_pairs={{0,12},{4,8},{8,4},{12,0},{1,13},{5,9},{9,5},{13,1},{2,14},{6,10},... | collective-permute-start | bytes 4718600 | tf_op jit(solution)/shard_map/ppermute | solution.py:28
  165.1 22.2 %collective-permute-start = (bf16[1024,448]{0,1:T(8,128)(2,1)S(1)}, bf16[1024,448]{0,1:T(8,128)(2,1)S(1)}, u32[]{:S(2)}, u32[]{:S(2)}) collective-permute-start(bf16[1024,448]{0,1:T(8,128)(2,1)S(1)} %concatenate.87), channel_id=1, source_target_pairs={{0,1},{1,0},{2,3},{3,2},{4,5},{5,4},{6,7},{7,6},{8,9},{9,8},{10,11... | collective-permute-start | bytes 2752520 | tf_op jit(solution)/shard_map/ppermute | solution.py:39
  185.9 25.0 %collective-permute-start.62 = (bf16[512,1024]{1,0:T(8,128)(2,1)S(1)}, bf16[512,1024]{1,0:T(8,128)(2,1)S(1)}, u32[]{:S(2)}, u32[]{:S(2)}) collective-permute-start(bf16[512,1024]{1,0:T(8,128)(2,1)S(1)} %bitcast.99), channel_id=1, source_target_pairs={{0,18},{2,16},{16,2},{18,0},{1,19},{3,17},{17,3},{19,1},{4,22},{6,... | collective-permute-start | bytes 3145736 | tf_op jit(solution)/shard_map/ppermute | solution.py:32
  187.4 24.4 %collective-permute-start.61 = (bf16[512,1024]{1,0:T(8,128)(2,1)S(1)}, bf16[512,1024]{1,0:T(8,128)(2,1)S(1)}, u32[]{:S(2)}, u32[]{:S(2)}) collective-permute-start(bf16[512,1024]{1,0:T(8,128)(2,1)S(1)} %bitcast.100), channel_id=1, source_target_pairs={{0,1},{1,0},{2,3},{3,2},{4,5},{5,4},{6,7},{7,6},{8,9},{9,8},{10,11... | collective-permute-start | bytes 3145736 | tf_op jit(solution)/shard_map/ppermute | solution.py:39
  188.7 44.8 %collective-permute-start.54 = (bf16[512,1024]{1,0:T(8,128)(2,1)S(1)}, bf16[512,1024]{1,0:T(8,128)(2,1)S(1)}, u32[]{:S(2)}, u32[]{:S(2)}) collective-permute-start(bf16[512,1024]{1,0:T(8,128)(2,1)S(1)} %bitcast.111), channel_id=1, source_target_pairs={{0,18},{2,16},{16,2},{18,0},{1,19},{3,17},{17,3},{19,1},{4,22},{6,... | collective-permute-start | bytes 3145736 | tf_op jit(solution)/shard_map/ppermute | solution.py:32
  193.7 47.3 %collective-permute-start.53 = (bf16[512,1024]{1,0:T(8,128)(2,1)S(1)}, bf16[512,1024]{1,0:T(8,128)(2,1)S(1)}, u32[]{:S(2)}, u32[]{:S(2)}) collective-permute-start(bf16[512,1024]{1,0:T(8,128)(2,1)S(1)} %bitcast.112), channel_id=1, source_target_pairs={{0,1},{1,0},{2,3},{3,2},{4,5},{5,4},{6,7},{7,6},{8,9},{9,8},{10,11... | collective-permute-start | bytes 3145736 | tf_op jit(solution)/shard_map/ppermute | solution.py:39
  197.5 58.5 %collective-permute-start.46 = (bf16[512,1024]{1,0:T(8,128)(2,1)S(1)}, bf16[512,1024]{1,0:T(8,128)(2,1)}, u32[]{:S(2)}, u32[]{:S(2)}) collective-permute-start(bf16[512,1024]{1,0:T(8,128)(2,1)S(1)} %bitcast.108), channel_id=1, source_target_pairs={{0,18},{2,16},{16,2},{18,0},{1,19},{3,17},{17,3},{19,1},{4,22},{6,... | collective-permute-start | bytes 3145736 | tf_op jit(solution)/shard_map/ppermute | solution.py:32
  211.0 46.8 %collective-permute-start.13 = (bf16[448,1024]{1,0:T(8,128)(2,1)S(1)}, bf16[448,1024]{1,0:T(8,128)(2,1)S(1)}, u32[]{:S(2)}, u32[]{:S(2)}) collective-permute-start(bf16[448,1024]{1,0:T(8,128)(2,1)S(1)} %pad_maximum_fusion.10.refs_1_), channel_id=1, source_target_pairs={{0,32},{32,64},{64,96},{96,0},{16,112},{48,16},{80,48},{112,80},{1... | collective-permute-start | bytes 2752520 | tf_op jit(solution)/shard_map/ppermute | solution.py:38
  211.7 46.8 %collective-permute-start.64 = (bf16[512,1024]{1,0:T(8,128)(2,1)S(1)}, bf16[512,1024]{1,0:T(8,128)(2,1)S(1)}, u32[]{:S(2)}, u32[]{:S(2)}) collective-permute-start(bf16[512,1024]{1,0:T(8,128)(2,1)S(1)} %collective-permute-done.62.refs_5_), channel_id=1, source_target_pairs={{0,32},{32,64},{64,96},{96,0},{16,112},{48,16},{80,48},{112,80},{1... | collective-permute-start | bytes 3145736 | tf_op jit(solution)/shard_map/ppermute | solution.py:38
  233.4 43.3 %collective-permute-start.56 = (bf16[512,1024]{1,0:T(8,128)(2,1)S(1)}, bf16[512,1024]{1,0:T(8,128)(2,1)S(1)}, u32[]{:S(2)}, u32[]{:S(2)}) collective-permute-start(bf16[512,1024]{1,0:T(8,128)(2,1)S(1)} %collective-permute-done.54.refs_5_), channel_id=1, source_target_pairs={{0,32},{32,64},{64,96},{96,0},{16,112},{48,16},{80,48},{112,80},{1... | collective-permute-start | bytes 3145736 | tf_op jit(solution)/shard_map/ppermute | solution.py:38
  241.0 47.3 %collective-permute-start.63 = (bf16[512,1024]{1,0:T(8,128)(2,1)S(1)}, bf16[512,1024]{1,0:T(8,128)(2,1)S(1)}, u32[]{:S(2)}, u32[]{:S(2)}) collective-permute-start(bf16[512,1024]{1,0:T(8,128)(2,1)S(1)} %collective-permute-done.62.refs_5_), channel_id=1, source_target_pairs={{0,1},{1,0},{2,3},{3,2},{4,5},{5,4},{6,7},{7,6},{8,9},{9,8},{10,11... | collective-permute-start | bytes 3145736 | tf_op jit(solution)/shard_map/ppermute | solution.py:39
  256.0 32.3 %collective-permute-start.55 = (bf16[512,1024]{1,0:T(8,128)(2,1)S(1)}, bf16[512,1024]{1,0:T(8,128)(2,1)S(1)}, u32[]{:S(2)}, u32[]{:S(2)}) collective-permute-start(bf16[512,1024]{1,0:T(8,128)(2,1)S(1)} %collective-permute-done.54.refs_5_), channel_id=1, source_target_pairs={{0,1},{1,0},{2,3},{3,2},{4,5},{5,4},{6,7},{7,6},{8,9},{9,8},{10,11... | collective-permute-start | bytes 3145736 | tf_op jit(solution)/shard_map/ppermute | solution.py:39
  257.8 41.5 %collective-permute-start.48 = (bf16[512,1024]{1,0:T(8,128)(2,1)}, bf16[512,1024]{1,0:T(8,128)(2,1)}, u32[]{:S(2)}, u32[]{:S(2)}) collective-permute-start(bf16[512,1024]{1,0:T(8,128)(2,1)} %collective-permute-done.46.refs_5_), channel_id=1, source_target_pairs={{0,32},{32,64},{64,96},{96,0},{16,112},{48,16},{80,48},{112,80},{1... | collective-permute-start | bytes 3145736 | tf_op jit(solution)/shard_map/ppermute | solution.py:38
  258.6 44.5 %collective-permute-start.65 = (bf16[512,1024]{1,0:T(8,128)(2,1)S(1)}, bf16[512,1024]{1,0:T(8,128)(2,1)S(1)}, u32[]{:S(2)}, u32[]{:S(2)}) collective-permute-start(bf16[512,1024]{1,0:T(8,128)(2,1)S(1)} %collective-permute-done.64.refs_7_), channel_id=1, source_target_pairs={{0,1},{1,0},{2,3},{3,2},{4,5},{5,4},{6,7},{7,6},{8,9},{9,8},{10,11... | collective-permute-start | bytes 3145736 | tf_op jit(solution)/shard_map/ppermute | solution.py:39
  276.7 26.4 %collective-permute-start.57 = (bf16[512,1024]{1,0:T(8,128)(2,1)S(1)}, bf16[512,1024]{1,0:T(8,128)(2,1)S(1)}, u32[]{:S(2)}, u32[]{:S(2)}) collective-permute-start(bf16[512,1024]{1,0:T(8,128)(2,1)S(1)} %collective-permute-done.56.refs_7_), channel_id=1, source_target_pairs={{0,1},{1,0},{2,3},{3,2},{4,5},{5,4},{6,7},{7,6},{8,9},{9,8},{10,11... | collective-permute-start | bytes 3145736 | tf_op jit(solution)/shard_map/ppermute | solution.py:39
  288.3 34.3 %collective-permute-start.45 = (bf16[512,1024]{1,0:T(8,128)(2,1)S(1)}, bf16[512,1024]{1,0:T(8,128)(2,1)}, u32[]{:S(2)}, u32[]{:S(2)}) collective-permute-start(bf16[512,1024]{1,0:T(8,128)(2,1)S(1)} %bitcast.109), channel_id=1, source_target_pairs={{0,1},{1,0},{2,3},{3,2},{4,5},{5,4},{6,7},{7,6},{8,9},{9,8},{10,11... | collective-permute-start | bytes 3145736 | tf_op jit(solution)/shard_map/ppermute | solution.py:39
  289.3 33.9 %collective-permute-start.38 = (bf16[512,1024]{1,0:T(8,128)(2,1)S(1)}, bf16[512,1024]{1,0:T(8,128)(2,1)S(1)}, u32[]{:S(2)}, u32[]{:S(2)}) collective-permute-start(bf16[512,1024]{1,0:T(8,128)(2,1)S(1)} %bitcast.105), channel_id=1, source_target_pairs={{0,18},{2,16},{16,2},{18,0},{1,19},{3,17},{17,3},{19,1},{4,22},{6,... | collective-permute-start | bytes 3145736 | tf_op jit(solution)/shard_map/ppermute | solution.py:32
  299.3 24.6 %collective-permute-start.47 = (bf16[512,1024]{1,0:T(8,128)(2,1)}, bf16[512,1024]{1,0:T(8,128)(2,1)}, u32[]{:S(2)}, u32[]{:S(2)}) collective-permute-start(bf16[512,1024]{1,0:T(8,128)(2,1)} %collective-permute-done.46.refs_5_), channel_id=1, source_target_pairs={{0,1},{1,0},{2,3},{3,2},{4,5},{5,4},{6,7},{7,6},{8,9},{9,8},{10,11... | collective-permute-start | bytes 3145736 | tf_op jit(solution)/shard_map/ppermute | solution.py:39
  303.0 20.8 %collective-permute-start.49 = (bf16[512,1024]{1,0:T(8,128)(2,1)}, bf16[512,1024]{1,0:T(8,128)(2,1)}, u32[]{:S(2)}, u32[]{:S(2)}) collective-permute-start(bf16[512,1024]{1,0:T(8,128)(2,1)} %collective-permute-done.48.refs_7_), channel_id=1, source_target_pairs={{0,1},{1,0},{2,3},{3,2},{4,5},{5,4},{6,7},{7,6},{8,9},{9,8},{10,11... | collective-permute-start | bytes 3145736 | tf_op jit(solution)/shard_map/ppermute | solution.py:39
  304.1 28.2 %collective-permute-start.5 = (f16[2,2,2,1,64,1152]{5,4,0,3,2,1:T(8,128)(2,1)}, f16[2,2,2,1,64,1152]{5,4,0,3,2,1:T(8,128)(2,1)}, u32[]{:S(2)}, u32[]{:S(2)}) collective-permute-start(f16[2,2,2,1,64,1152]{5,4,0,3,2,1:T(8,128)(2,1)} %copy.72), channel_id=1, source_target_pairs={{0,4},{4,0},{8,12},{12,8},{1,5},{5,1},{9,13},{13,9},{2,6},{6,2},{1... | collective-permute-start | bytes 3538952 | tf_op jit(solution)/shard_map/ppermute | solution.py:26
  322.6 96.7 %collective-permute-start.37 = (bf16[512,1024]{1,0:T(8,128)(2,1)S(1)}, bf16[512,1024]{1,0:T(8,128)(2,1)S(1)}, u32[]{:S(2)}, u32[]{:S(2)}) collective-permute-start(bf16[512,1024]{1,0:T(8,128)(2,1)S(1)} %bitcast.106), channel_id=1, source_target_pairs={{0,1},{1,0},{2,3},{3,2},{4,5},{5,4},{6,7},{7,6},{8,9},{9,8},{10,11... | collective-permute-start | bytes 3145736 | tf_op jit(solution)/shard_map/ppermute | solution.py:39
  323.2 97.5 %collective-permute-start.24 = (bf16[512,1024]{1,0:T(8,128)(2,1)S(1)}, bf16[512,1024]{1,0:T(8,128)(2,1)S(1)}, u32[]{:S(2)}, u32[]{:S(2)}) collective-permute-start(bf16[512,1024]{1,0:T(8,128)(2,1)S(1)} %bitcast.102), channel_id=1, source_target_pairs={{0,18},{2,16},{16,2},{18,0},{1,19},{3,17},{17,3},{19,1},{4,22},{6,... | collective-permute-start | bytes 3145736 | tf_op jit(solution)/shard_map/ppermute | solution.py:32
  323.8 95.6 %collective-permute-start.40 = (bf16[512,1024]{1,0:T(8,128)(2,1)S(1)}, bf16[512,1024]{1,0:T(8,128)(2,1)S(1)}, u32[]{:S(2)}, u32[]{:S(2)}) collective-permute-start(bf16[512,1024]{1,0:T(8,128)(2,1)S(1)} %collective-permute-done.38.refs_5_), channel_id=1, source_target_pairs={{0,32},{32,64},{64,96},{96,0},{16,112},{48,16},{80,48},{112,80},{1... | collective-permute-start | bytes 3145736 | tf_op jit(solution)/shard_map/ppermute | solution.py:38
  323.8 38.6 %collective-permute-start.2 = (f16[2,1,2,2,64,1280]{5,4,0,3,2,1:T(8,128)(2,1)}, f16[2,1,2,2,64,1280]{5,4,0,3,2,1:T(8,128)(2,1)S(1)}, u32[]{:S(2)}, u32[]{:S(2)}) collective-permute-start(f16[2,1,2,2,64,1280]{5,4,0,3,2,1:T(8,128)(2,1)} %copy.70), channel_id=1, source_target_pairs={{0,2},{2,0},{1,3},{3,1},{4,6},{6,4},{5,7},{7,5},{8,10},{10,8},{9,1... | collective-permute-start | bytes 3932168 | tf_op jit(solution)/shard_map/ppermute | solution.py:30
  332.3 28.1 %collective-permute-start.8 = (f16[2,2,1,2,64,1152]{5,4,0,3,2,1:T(8,128)(2,1)}, f16[2,2,1,2,64,1152]{5,4,0,3,2,1:T(8,128)(2,1)S(1)}, u32[]{:S(2)}, u32[]{:S(2)}) collective-permute-start(f16[2,2,1,2,64,1152]{5,4,0,3,2,1:T(8,128)(2,1)} %copy.74), channel_id=1, source_target_pairs={{0,12},{4,8},{8,4},{12,0},{1,13},{5,9},{9,5},{13,1},{2,14},{6,10},... | collective-permute-start | bytes 3538952 | tf_op jit(solution)/shard_map/ppermute | solution.py:28
  360.4 13.5 %collective-permute-start.6 = (f16[2,1,2,1,64,1152]{5,4,0,3,2,1:T(8,128)(2,1)S(1)}, f16[2,1,2,1,64,1152]{5,4,0,3,2,1:T(8,128)(2,1)S(1)}, u32[]{:S(2)}, u32[]{:S(2)}) collective-permute-start(f16[2,1,2,1,64,1152]{5,4,0,3,2,1:T(8,128)(2,1)S(1)} %slice_convert_fusion.2), channel_id=1, source_target_pairs={{0,2},{2,0},{1,3},{3,1},{4,6},{6,4},{5,7},{7,5},{8,10},{10,8},{9,1... | collective-permute-start | bytes 1769480 | tf_op jit(solution)/shard_map/ppermute | solution.py:30
  362.5 14.0 %collective-permute-start.9 = (f16[2,2,1,1,64,1152]{5,4,0,3,2,1:T(8,128)(2,1)S(1)}, f16[2,2,1,1,64,1152]{5,4,0,3,2,1:T(8,128)(2,1)S(1)}, u32[]{:S(2)}, u32[]{:S(2)}) collective-permute-start(f16[2,2,1,1,64,1152]{5,4,0,3,2,1:T(8,128)(2,1)S(1)} %slice_convert_fusion.1), channel_id=1, source_target_pairs={{0,4},{4,0},{8,12},{12,8},{1,5},{5,1},{9,13},{13,9},{2,6},{6,2},{1... | collective-permute-start | bytes 1769480 | tf_op jit(solution)/shard_map/ppermute | solution.py:26
  373.9 74.9 %collective-permute-start.33 = (bf16[3,512,1024]{2,1,0:T(8,128)(2,1)}, bf16[3,512,1024]{2,1,0:T(8,128)(2,1)}, u32[]{:S(2)}, u32[]{:S(2)}) collective-permute-start(bf16[3,512,1024]{2,1,0:T(8,128)(2,1)} %bitcast.48), channel_id=1, source_target_pairs={{0,1},{1,0},{2,3},{3,2},{4,5},{5,4},{6,7},{7,6},{8,9},{9,8},{10,11... | collective-permute-start | bytes 9437192 | tf_op jit(solution)/shard_map/ppermute | solution.py:39
  376.5 16.5 %collective-permute-start.3 = (f16[2,1,1,2,64,1280]{5,4,0,3,2,1:T(8,128)(2,1)S(1)}, f16[2,1,1,2,64,1280]{5,4,0,3,2,1:T(8,128)(2,1)S(1)}, u32[]{:S(2)}, u32[]{:S(2)}) collective-permute-start(f16[2,1,1,2,64,1280]{5,4,0,3,2,1:T(8,128)(2,1)S(1)} %slice_convert_fusion), channel_id=1, source_target_pairs={{0,12},{4,8},{8,4},{12,0},{1,13},{5,9},{9,5},{13,1},{2,14},{6,10},... | collective-permute-start | bytes 1966088 | tf_op jit(solution)/shard_map/ppermute | solution.py:28
  393.0 7.4 %collective-permute-start.7 = (f16[2,1,1,1,64,1152]{5,4,0,3,2,1:T(8,128)(2,1)S(1)}, f16[2,1,1,1,64,1152]{5,4,0,3,2,1:T(8,128)(2,1)S(1)}, u32[]{:S(2)}, u32[]{:S(2)}) collective-permute-start(f16[2,1,1,1,64,1152]{5,4,0,3,2,1:T(8,128)(2,1)S(1)} %slice_convert_fusion.5), channel_id=1, source_target_pairs={{0,12},{4,8},{8,4},{12,0},{1,13},{5,9},{9,5},{13,1},{2,14},{6,10},... | collective-permute-start | bytes 884744 | tf_op jit(solution)/shard_map/ppermute | solution.py:28
  400.4 8.6 %collective-permute-start.10 = (f16[2,1,1,1,64,1152]{5,4,0,3,2,1:T(8,128)(2,1)S(1)}, f16[2,1,1,1,64,1152]{5,4,0,3,2,1:T(8,128)(2,1)S(1)}, u32[]{:S(2)}, u32[]{:S(2)}) collective-permute-start(f16[2,1,1,1,64,1152]{5,4,0,3,2,1:T(8,128)(2,1)S(1)} %slice_convert_fusion.4), channel_id=1, source_target_pairs={{0,2},{2,0},{1,3},{3,1},{4,6},{6,4},{5,7},{7,5},{8,10},{10,8},{9,1... | collective-permute-start | bytes 884744 | tf_op jit(solution)/shard_map/ppermute | solution.py:30
  409.0 6.6 %collective-permute-start.4 = (f16[2,1,1,1,64,1280]{5,4,0,3,2,1:T(8,128)(2,1)S(1)}, f16[2,1,1,1,64,1280]{5,4,0,3,2,1:T(8,128)(2,1)S(1)}, u32[]{:S(2)}, u32[]{:S(2)}) collective-permute-start(f16[2,1,1,1,64,1280]{5,4,0,3,2,1:T(8,128)(2,1)S(1)} %slice_convert_fusion.3), channel_id=1, source_target_pairs={{0,4},{4,0},{8,12},{12,8},{1,5},{5,1},{9,13},{13,9},{2,6},{6,2},{1... | collective-permute-start | bytes 983048 | tf_op jit(solution)/shard_map/ppermute | solution.py:26
  415.6 35.3 %collective-permute-start.19 = (bf16[3,512,1024]{2,1,0:T(8,128)(2,1)}, bf16[3,512,1024]{2,1,0:T(8,128)(2,1)}, u32[]{:S(2)}, u32[]{:S(2)}) collective-permute-start(bf16[3,512,1024]{2,1,0:T(8,128)(2,1)} %bitcast.37), channel_id=1, source_target_pairs={{0,1},{1,0},{2,3},{3,2},{4,5},{5,4},{6,7},{7,6},{8,9},{9,8},{10,11... | collective-permute-start | bytes 9437192 | tf_op jit(solution)/shard_map/ppermute | solution.py:39
  419.3 6.6 %collective-permute-start.39 = (bf16[512,1024]{1,0:T(8,128)(2,1)S(1)}, bf16[512,1024]{1,0:T(8,128)(2,1)S(1)}, u32[]{:S(2)}, u32[]{:S(2)}) collective-permute-start(bf16[512,1024]{1,0:T(8,128)(2,1)S(1)} %collective-permute-done.38.refs_5_), channel_id=1, source_target_pairs={{0,1},{1,0},{2,3},{3,2},{4,5},{5,4},{6,7},{7,6},{8,9},{9,8},{10,11... | collective-permute-start | bytes 3145736 | tf_op jit(solution)/shard_map/ppermute | solution.py:39
  419.4 8.1 %collective-permute-start.41 = (bf16[512,1024]{1,0:T(8,128)(2,1)S(1)}, bf16[512,1024]{1,0:T(8,128)(2,1)S(1)}, u32[]{:S(2)}, u32[]{:S(2)}) collective-permute-start(bf16[512,1024]{1,0:T(8,128)(2,1)S(1)} %collective-permute-done.40.refs_7_), channel_id=1, source_target_pairs={{0,1},{1,0},{2,3},{3,2},{4,5},{5,4},{6,7},{7,6},{8,9},{9,8},{10,11... | collective-permute-start | bytes 3145736 | tf_op jit(solution)/shard_map/ppermute | solution.py:39
  420.7 26.0 %collective-permute-start.26 = (bf16[512,1024]{1,0:T(8,128)(2,1)S(1)}, bf16[512,1024]{1,0:T(8,128)(2,1)S(1)}, u32[]{:S(2)}, u32[]{:S(2)}) collective-permute-start(bf16[512,1024]{1,0:T(8,128)(2,1)S(1)} %collective-permute-done.24.refs_5_), channel_id=1, source_target_pairs={{0,32},{32,64},{64,96},{96,0},{16,112},{48,16},{80,48},{112,80},{1... | collective-permute-start | bytes 3145736 | tf_op jit(solution)/shard_map/ppermute | solution.py:38
  425.9 34.9 %collective-permute-start.23 = (bf16[512,1024]{1,0:T(8,128)(2,1)S(1)}, bf16[512,1024]{1,0:T(8,128)(2,1)S(1)}, u32[]{:S(2)}, u32[]{:S(2)}) collective-permute-start(bf16[512,1024]{1,0:T(8,128)(2,1)S(1)} %bitcast.103), channel_id=1, source_target_pairs={{0,1},{1,0},{2,3},{3,2},{4,5},{5,4},{6,7},{7,6},{8,9},{9,8},{10,11... | collective-permute-start | bytes 3145736 | tf_op jit(solution)/shard_map/ppermute | solution.py:39
  427.5 20.1 %collective-permute-start.11 = (bf16[64,3584]{1,0:T(8,128)(2,1)S(1)}, bf16[64,3584]{1,0:T(8,128)(2,1)S(1)}, u32[]{:S(2)}, u32[]{:S(2)}) collective-permute-start(bf16[64,3584]{1,0:T(8,128)(2,1)S(1)} %get-tuple-element.50), channel_id=1, source_target_pairs={{0,1},{1,0},{2,3},{3,2},{4,5},{5,4},{6,7},{7,6},{8,9},{9,8},{10,11... | collective-permute-start | bytes 1376264 | tf_op jit(solution)/shard_map/ppermute | solution.py:39
  446.7 14.0 %collective-permute-start.25 = (bf16[512,1024]{1,0:T(8,128)(2,1)S(1)}, bf16[512,1024]{1,0:T(8,128)(2,1)S(1)}, u32[]{:S(2)}, u32[]{:S(2)}) collective-permute-start(bf16[512,1024]{1,0:T(8,128)(2,1)S(1)} %collective-permute-done.24.refs_5_), channel_id=1, source_target_pairs={{0,1},{1,0},{2,3},{3,2},{4,5},{5,4},{6,7},{7,6},{8,9},{9,8},{10,11... | collective-permute-start | bytes 3145736 | tf_op jit(solution)/shard_map/ppermute | solution.py:39
  447.6 13.2 %collective-permute-start.27 = (bf16[512,1024]{1,0:T(8,128)(2,1)S(1)}, bf16[512,1024]{1,0:T(8,128)(2,1)S(1)}, u32[]{:S(2)}, u32[]{:S(2)}) collective-permute-start(bf16[512,1024]{1,0:T(8,128)(2,1)S(1)} %collective-permute-done.26.refs_7_), channel_id=1, source_target_pairs={{0,1},{1,0},{2,3},{3,2},{4,5},{5,4},{6,7},{7,6},{8,9},{9,8},{10,11... | collective-permute-start | bytes 3145736 | tf_op jit(solution)/shard_map/ppermute | solution.py:39
  (50 other events, 836.6 us)
